TPU v7x, 128 devices: a whole 4x4x4 slice. The times are simulated.
128 devices in a mesh: occ: 16 (over x_lo, z, core), aux: 8 (over x_hi, y).
Axes of the slice: x: 4 (x_hi: 2, x_lo: 2; x = x_hi * 2 + x_lo), y: 4, z: 4, core: 2. Of those that a mesh axis runs over, the one named last changes fastest.
Arguments:
- orbital_b: bfloat16 [48, 256, 12288], P('occ', None, 'aux'), may hold values from -0.109375 to 0.109375
- block_size: int32 [16], replicated, may hold values from 1 to 3, 32 in all
- occ_energy: float32 [48], replicated, may hold values from -1.5 to -0.5
- virt_energy: float32 [256], replicated, may hold values from 0.2 to 1.2
Outputs:
- gamma: float32 [48, 256, 12288], P('occ', None, 'aux')
Inputs may be any that keep to these rules, and one draw needn't show every extreme that they name: `block_size`: the sizes sum to 32; the largest is exactly 3.
All inputs are finite; a program needn't handle non-finite values.
Results may differ from a plain program's by a relative error of at most 0.0024.
Values may be sent and summed in bfloat16 or wider, within the bound.
A program may use at most 128 MiB of HBM per device.

v0:
```python
import jax
import jax.numpy as jnp
from jax import lax
from jax.sharding import PartitionSpec as P

STEPS = 4


def from_behind(value, axis, steps):
    count = lax.axis_size(axis)
    pairs = [(source, (source + steps) % count) for source in range(count)]
    return lax.ppermute(value, axis, pairs)


def per_device(orbital_b, block_size, occ_energy, virt_energy):
    slots = orbital_b.shape[0]
    virtuals = orbital_b.shape[1]
    shard = orbital_b.shape[2]
    n_blocks = lax.axis_size("occ")
    here = lax.axis_index("occ")
    valid = jnp.arange(slots, dtype=jnp.int32) < block_size[here]
    own = jnp.where(valid[:, None, None], orbital_b, jnp.zeros_like(orbital_b)).reshape(
        slots * virtuals, shard
    )

    def row_energy(block):
        block_e = lax.dynamic_slice_in_dim(occ_energy, block * slots, slots)
        return (virt_energy[None, :] - block_e[:, None]).reshape(slots * virtuals)

    own_rows = row_energy(here)
    gamma = jnp.zeros((slots * virtuals, shard), jnp.float32)
    slab = own
    for offset in range(STEPS):
        if offset > 0:
            slab = from_behind(slab, "occ", 1)
        source = (here - offset) % n_blocks
        col_rows = row_energy(source)
        product = lax.dot_general(
            own, slab, (((1,), (1,)), ((), ())), preferred_element_type=jnp.float32
        )
        total = lax.psum(product, "aux")
        amp = (total / (own_rows[:, None] + col_rows[None, :])).astype(jnp.bfloat16)
        gamma = gamma + jnp.dot(amp, slab, preferred_element_type=jnp.float32)
        if offset > 0:
            partial_back = lax.dot_general(
                amp, own, (((0,), (0,)), ((), ())), preferred_element_type=jnp.float32
            )
            gamma = gamma + from_behind(partial_back, "occ", -offset)
    return gamma.reshape(slots, virtuals, shard)


def solution(mesh):
    in_specs = (P("occ", None, "aux"), P(), P(), P())
    out_specs = P("occ", None, "aux")
    return jax.shard_map(
        per_device, mesh=mesh, in_specs=in_specs, out_specs=out_specs, check_vma=False
    )
```

profile of v0, /device:TPU:96, one launch (start us, length us, event | category | flops | bytes accessed | tf_op | source)
XLA Modules:
  0.0 603.7 jit_solution(7748287506985308704)
XLA Ops:
  6.5 0.0 all-reduce.3.cloned.1.call-start
  6.5 1.2 dynamic_slice.18
  7.8 0.6 iota_compare_fusion
  8.4 1.9 broadcast_select_fusion
  10.3 0.1 collective-permute-start
  10.4 28.3 %collective-permute-done = bf16[768,1536]{1,0:T(8,128)(2,1)S(1)} collective-permute-done((bf16[768,1536]{1,0:T(8,128)(2,1)S(1)}, bf16[768,1536]{1,0:T(8,128)(2,1)S(1)}, u32[]{:S(2)}, u32[]{:S(2)}) %collective-permute-start) | collective-permute-done | bytes 2359328 | tf_op jit(solution)/shard_map/ppermute | solution.py:12
  38.7 0.0 copy-start.3
  38.7 0.0 collective-permute-start.2
  38.7 28.3 %collective-permute-done.2 = bf16[768,1536]{1,0:T(8,128)(2,1)S(1)} collective-permute-done((bf16[768,1536]{1,0:T(8,128)(2,1)S(1)}, bf16[768,1536]{1,0:T(8,128)(2,1)S(1)}, u32[]{:S(2)}, u32[]{:S(2)}) %collective-permute-start.2) | collective-permute-done | bytes 2359328 | tf_op jit(solution)/shard_map/ppermute | solution.py:12
  66.9 0.0 copy-start.5
  66.9 0.0 collective-permute-start.4
  66.9 3.5 fusion.9
  70.4 0.0 copy-done.3
  70.4 3.4 fusion.10
  73.9 0.0 copy-done.5
  73.9 3.4 fusion.11
  77.3 17.9 %collective-permute-done.4 = bf16[768,1536]{1,0:T(8,128)(2,1)S(1)} collective-permute-done((bf16[768,1536]{1,0:T(8,128)(2,1)S(1)}, bf16[768,1536]{1,0:T(8,128)(2,1)S(1)}, u32[]{:S(2)}, u32[]{:S(2)}) %collective-permute-start.4) | collective-permute-done | bytes 2359328 | tf_op jit(solution)/shard_map/ppermute | solution.py:12
  95.2 0.0 copy-start
  95.2 1.4 copy-done
  96.6 3.4 fusion.12
  100.0 0.0 copy-start.1
  100.0 0.0 copy-start.2
  100.0 0.0 all-reduce.3.cloned.1.call-update
  100.1 0.5 copy-done.1
  100.7 0.1 fusion.8
  100.8 0.0 copy-done.2
  100.8 0.1 broadcast_subtract_fusion.3
  100.9 210.4 %all-reduce.3.cloned.1.call-done = (f32[768,768]{1,0:T(8,128)}, f32[768,768]{1,0:T(8,128)}, f32[768,768]{1,0:T(8,128)}, f32[768,768]{1,0:T(8,128)}) async-done(((f32[768,768]{1,0:T(8,128)}, f32[768,768]{1,0:T(8,128)}, f32[768,768]{1,0:T(8,128)}, f32[768,768]{1,0:T(8,128)}), (f32[768,768]{1,0:T(8,128)}, f32[768,768]{1,0:T(8,128)}, f32[768,768]{1,0:T(8,128)}, ...) | async-done | bytes 9437200 | tf_op jit(solution)/shard_map/psum | solution.py:41
  311.3 0.0 copy-start.7
  311.3 6.2 %fusion.7 = f32[768,1536]{1,0:T(8,128)} fusion(bf16[768,1536]{1,0:T(8,128)(2,1)S(1)} %bitcast.23, f32[768,768]{1,0:T(8,128)} %get-tuple-element.5, f32[768]{0:T(1024)S(1)} %sub.119, f32[768]{0:T(1024)S(1)} %sub.104), kind=kOutput, calls=%fused_computation.19 | convolution fusion | flops 1813708800 | bytes 9443328 | tf_op jit(solution)/shard_map/dot_general | solution.py:45
  317.5 0.7 collective-permute-start.5
  318.2 0.0 copy-done.7
  318.2 0.0 copy-start.9
  318.2 4.4 fusion.3
  322.6 0.3 collective-permute-start.1
  322.9 0.0 copy-done.9
  322.9 4.5 fusion.5
  327.4 0.5 collective-permute-start.3
  327.8 0.0 copy-start.6
  327.8 0.0 copy-start.10
  327.8 4.0 fusion
  331.8 0.0 copy-done.6
  331.8 0.0 copy-done.10
  331.8 0.0 copy-start.4
  331.8 0.0 copy-start.8
  331.8 2.2 fusion.6
  334.0 0.0 copy-done.4
  334.0 0.2 copy-done.8
  334.2 2.1 fusion.4
  336.3 96.7 %collective-permute-done.5 = f32[768,1536]{1,0:T(8,128)} collective-permute-done((f32[768,1536]{1,0:T(8,128)}, f32[768,1536]{1,0:T(8,128)}, u32[]{:S(2)}, u32[]{:S(2)}) %collective-permute-start.5) | collective-permute-done | bytes 4718624 | tf_op jit(solution)/shard_map/ppermute | solution.py:12
  433.0 88.3 %collective-permute-done.1 = f32[768,1536]{1,0:T(8,128)} collective-permute-done((f32[768,1536]{1,0:T(8,128)}, f32[768,1536]{1,0:T(8,128)}, u32[]{:S(2)}, u32[]{:S(2)}) %collective-permute-start.1) | collective-permute-done | bytes 4718624 | tf_op jit(solution)/shard_map/ppermute | solution.py:12
  521.3 63.5 %collective-permute-done.3 = f32[768,1536]{1,0:T(8,128)} collective-permute-done((f32[768,1536]{1,0:T(8,128)}, f32[768,1536]{1,0:T(8,128)}, u32[]{:S(2)}, u32[]{:S(2)}) %collective-permute-start.3) | collective-permute-done | bytes 4718624 | tf_op jit(solution)/shard_map/ppermute | solution.py:12
  584.9 12.0 %add_add_fusion = f32[768,1536]{1,0:T(8,128)} fusion(f32[768,1536]{1,0:T(8,128)} %collective-permute-done.5, f32[768,1536]{1,0:T(8,128)} %collective-permute-done.3, f32[768,1536]{1,0:T(8,128)S(1)} %fusion.6, f32[768,1536]{1,0:T(8,128)} %collective-permute-done.1, f32[768,1536]{1,0:T(8,128)S(1)} %fusion, f32[768,1536]{1,0:T(8,128)S(1)} %fusion.4, ...), kind=kOutput, calls=%fused_computation | convolution fusion | flops 1820786688 | bytes 37754880 | tf_op jit(solution)/shard_map/dot_general | solution.py:43
  (5 shorter events, 0.0 us)
Async XLA Ops:
  6.5 304.7 %all-reduce.3.cloned.1.call-start = ((), (), s32[]{:S(2)}) async-start(), calls=%async_computation | async-start | bytes 18874368 | tf_op jit(solution)/shard_map/psum | solution.py:41
  10.3 28.3 %collective-permute-start = (bf16[768,1536]{1,0:T(8,128)(2,1)S(1)}, bf16[768,1536]{1,0:T(8,128)(2,1)S(1)}, u32[]{:S(2)}, u32[]{:S(2)}) collective-permute-start(bf16[768,1536]{1,0:T(8,128)(2,1)S(1)} %bitcast.18), channel_id=1, source_target_pairs={{0,8},{8,16},{16,24},{24,32},{32,40},{40,48},{48,56},{56,64},{64,7... | collective-permute-start | bytes 7077896 | tf_op jit(solution)/shard_map/ppermute | solution.py:12
  38.7 31.7 %copy-start.3 = (bf16[768,1536]{1,0:T(8,128)(2,1)}, bf16[768,1536]{1,0:T(8,128)(2,1)S(1)}, u32[]{:S(2)}) copy-start(bf16[768,1536]{1,0:T(8,128)(2,1)S(1)} %collective-permute-done) | copy-start | bytes 7077892
  38.7 28.3 %collective-permute-start.2 = (bf16[768,1536]{1,0:T(8,128)(2,1)S(1)}, bf16[768,1536]{1,0:T(8,128)(2,1)S(1)}, u32[]{:S(2)}, u32[]{:S(2)}) collective-permute-start(bf16[768,1536]{1,0:T(8,128)(2,1)S(1)} %collective-permute-done), channel_id=1, source_target_pairs={{0,8},{8,16},{16,24},{24,32},{32,40},{40,48},{48,56},{56,64},{64,7... | collective-permute-start | bytes 7077896 | tf_op jit(solution)/shard_map/ppermute | solution.py:12
  66.9 6.9 %copy-start.5 = (bf16[768,1536]{1,0:T(8,128)(2,1)}, bf16[768,1536]{1,0:T(8,128)(2,1)S(1)}, u32[]{:S(2)}) copy-start(bf16[768,1536]{1,0:T(8,128)(2,1)S(1)} %collective-permute-done.2) | copy-start | bytes 7077892
  66.9 28.3 %collective-permute-start.4 = (bf16[768,1536]{1,0:T(8,128)(2,1)S(1)}, bf16[768,1536]{1,0:T(8,128)(2,1)S(1)}, u32[]{:S(2)}, u32[]{:S(2)}) collective-permute-start(bf16[768,1536]{1,0:T(8,128)(2,1)S(1)} %collective-permute-done.2), channel_id=1, source_target_pairs={{0,8},{8,16},{16,24},{24,32},{32,40},{40,48},{48,56},{56,64},{64,7... | collective-permute-start | bytes 7077896 | tf_op jit(solution)/shard_map/ppermute | solution.py:12
  95.2 1.4 copy-start
  100.0 0.7 copy-start.1
  100.0 0.7 copy-start.2
  311.3 6.9 %copy-start.7 = (f32[768,768]{1,0:T(8,128)S(1)}, f32[768,768]{1,0:T(8,128)}, u32[]{:S(2)}) copy-start(f32[768,768]{1,0:T(8,128)} %get-tuple-element.7) | copy-start | bytes 7077892
  317.5 115.5 %collective-permute-start.5 = (f32[768,1536]{1,0:T(8,128)}, f32[768,1536]{1,0:T(8,128)}, u32[]{:S(2)}, u32[]{:S(2)}) collective-permute-start(f32[768,1536]{1,0:T(8,128)} %fusion.7), channel_id=1, source_target_pairs={{0,104},{8,112},{16,120},{24,0},{32,8},{40,16},{48,24},{56,32},{64... | collective-permute-start | bytes 14155784 | tf_op jit(solution)/shard_map/ppermute | solution.py:12
  318.2 4.7 copy-start.9
  322.6 198.7 %collective-permute-start.1 = (f32[768,1536]{1,0:T(8,128)}, f32[768,1536]{1,0:T(8,128)}, u32[]{:S(2)}, u32[]{:S(2)}) collective-permute-start(f32[768,1536]{1,0:T(8,128)} %fusion.3), channel_id=1, source_target_pairs={{0,120},{8,0},{16,8},{24,16},{32,24},{40,32},{48,40},{56,48},{64,5... | collective-permute-start | bytes 14155784 | tf_op jit(solution)/shard_map/ppermute | solution.py:12
  327.4 257.5 %collective-permute-start.3 = (f32[768,1536]{1,0:T(8,128)}, f32[768,1536]{1,0:T(8,128)}, u32[]{:S(2)}, u32[]{:S(2)}) collective-permute-start(f32[768,1536]{1,0:T(8,128)} %fusion.5), channel_id=1, source_target_pairs={{0,112},{8,120},{16,0},{24,8},{32,16},{40,24},{48,32},{56,40},{64,... | collective-permute-start | bytes 14155784 | tf_op jit(solution)/shard_map/ppermute | solution.py:12
  327.8 4.0 copy-start.6
  327.8 4.0 copy-start.10
  331.8 2.2 copy-start.4
  331.8 2.4 copy-start.8
Sparse Core Ops, SparseCore 0:
  100.2 211.0 all-reduce.2
where the time goes:
time: 604 us
  waiting for transfers between devices  533 us (88%)
  matrix products  49.1 us (8%)
  between operations  13.6 us (2%)
    ppermute x6, waiting for transfers between devices, from_behind(): return lax.ppermute(value, axis, pairs)  323 us
    psum x1, waiting for transfers between devices, per_device(): total = lax.psum(product, 'aux')  210 us
    dot_general x4, matrix products, per_device(): gamma = gamma + jnp.dot(amp, slab, preferred_element_type=jnp.float32)  20.2 us
    dot_general x3, matrix products, per_device(): lax.dot_general(amp, own, (((0,), (0,)), ((), ())), preferred_element_typ...  15.1 us
    dot_general x4, matrix products, per_device(): lax.dot_general(own, slab, (((1,), (1,)), ((), ())), preferred_element_ty...  13.8 us
  transfers between devices with their start and end apart: 7, of which 7 were waited for; matrix products, arithmetic and copies ran while one was open for 5% of the time, Pallas kernels for 0%

commit v1 on v0

v1 whole, which is shorter than its diff:
```python
import jax
import jax.numpy as jnp
from jax import lax
from jax.experimental import pallas as pl
from jax.experimental.pallas import tpu as pltpu
from jax.sharding import PartitionSpec as P

MESH = pl.DeviceIdType.MESH
BF16 = jnp.bfloat16
F32 = jnp.float32

SLAB_SHIFT = (0, 1, -1, -2, 2, 3)
PAIRS = ((0, 0), (1, 1), (1, 0), (0, 2), (1, 2), (4, 0), (4, 2), (1, 3))
N_PAIR = len(PAIRS)

STAGE_AT = dict(P=0.0, Q=2.5, R=5.5, T=10.0, U=14.0, V=17.0, W=20.0, Y=24.0, Z=27.0)
START = {0: 0.0, 2: 4.0, 1: 8.0, 5: 20.0, 3: 24.0, 6: 28.0, 4: 32.0, 7: 46.0}


def schedule():
    events = []
    for pair, begin in START.items():
        for stage, offset in STAGE_AT.items():
            events.append((begin + offset, stage, pair))
    for stage in "UVWYZ":
        events.append((START[7] + STAGE_AT[stage] + 3.0, stage, 8))
    return [(stage, pair) for _, stage, pair in sorted(events)]


def rows(start, size, align=16):
    return pl.ds(pl.multiple_of(start, align), size)


def kernel(orb, sizes, occ_e, virt, out, swap, slab, own, give, half, c1, d1, c2, e2, f2, amp,
           gam, bsend, brecv, vcol, s_swap, s_slab, s_half, s_c1, s_c2, s_f, s_ax, s_ay, s_fw,
           s_sib, s_z8, s_back, s_out):
    o = lax.axis_index("occ")
    a = lax.axis_index("aux")
    chip, core = o // 2, o % 2
    xh, y = a // 4, a % 4
    sibling = (chip * 2 + 1 - core, a)
    above = (((chip + 1) % 8) * 2 + core, a)
    below = (((chip + 7) % 8) * 2 + core, a)
    yup = (o, xh * 4 + (y + 1) % 4)
    ydn = (o, xh * 4 + (y + 3) % 4)
    xpart = (o, (1 - xh) * 4 + y)
    partners = (sibling, above, below, yup, ydn, xpart)

    barrier = pltpu.get_barrier_semaphore()
    for device in partners:
        pl.semaphore_signal(barrier, inc=1, device_id=device, device_id_type=MESH)
    pl.semaphore_wait(barrier, len(partners))

    pending = []

    def remote(src, dst, sems, device):
        copy = pltpu.make_async_remote_copy(
            src_ref=src, dst_ref=dst, send_sem=sems[0], recv_sem=sems[1], device_id=device,
            device_id_type=MESH)
        return copy

    def send(src, dst, sems, device):
        copy = remote(src, dst, sems, device)
        copy.start()
        pending.append(copy)
        return copy

    def landed(dst, sems):
        remote(dst, dst, sems, sibling).wait_recv()

    def pairsem(sem, *index):
        return sem.at[(0,) + index], sem.at[(1,) + index]

    mine = pl.ds(pl.multiple_of(core * 768, 128), 768)
    other = pl.ds(pl.multiple_of((1 - core) * 768, 128), 768)
    live = sizes[o]

    def mask_other(i, _):
        r = rows(i * 64, 64)
        swap[r, :] = jnp.where(i // 4 < live, orb[r, other], jnp.zeros((64, 768), BF16))
        return 0

    def mask_mine(i, _):
        r = rows(i * 64, 64)
        slab[core, r, :] = jnp.where(i // 4 < live, orb[r, mine], jnp.zeros((64, 768), BF16))
        return 0

    lax.fori_loop(0, 12, mask_other, 0)
    send(swap, slab.at[core], pairsem(s_swap), sibling)
    lax.fori_loop(0, 12, mask_mine, 0)

    column = jnp.broadcast_to(virt[...], (128, 256)).T
    vcol[0:256, :] = column
    vcol[256:512, :] = column

    landed(slab.at[1 - core], pairsem(s_swap))
    send(slab.at[1], slab.at[2], pairsem(s_slab, 0), above)
    send(slab.at[0], slab.at[4], pairsem(s_slab, 1), below)

    arrived = set()

    def need(index):
        if index < 2 or index in arrived:
            return
        if index in (2, 4):
            landed(slab.at[index], pairsem(s_slab, (index - 2) // 2))
            if index == 2:
                send(slab.at[0], slab.at[3], pairsem(s_slab, 2), above)
            else:
                send(slab.at[1], slab.at[5], pairsem(s_slab, 3), below)
        else:
            landed(slab.at[index], pairsem(s_slab, 2 + (index - 3) // 2))
        arrived.add(index)

    base = core * 384
    r_own = y * 96
    r_up = ((y + 1) % 4) * 96
    r_dn = ((y + 3) % 4) * 96
    r_far = ((y + 2) % 4) * 96
    gives = {}

    def stage_p(b):
        left, right = PAIRS[b]
        need(left)
        need(right)
        slot = b % 3
        if slot in gives:
            gives[slot].wait_send()

        def product(dst, first):
            def column_tile(n, _):
                dst[slot, :, pl.ds(pl.multiple_of(n * 256, 256), 256)] = lax.dot_general(
                    slab[left, rows(first, 384), :], slab[right, rows(n * 256, 256), :],
                    (((1,), (1,)), ((), ())), preferred_element_type=F32)
                return 0
            lax.fori_loop(0, 3, column_tile, 0)

        product(give, 384 - base)
        gives[slot] = remote(give.at[slot], half.at[b], pairsem(s_half, b), sibling)
        gives[slot].start()
        product(own, base)

    def stage_q(b):
        slot = b % 3
        landed(half.at[b], pairsem(s_half, b))

        def far(i, _):
            r = rows(r_far + i * 48, 48)
            c1[b, rows(i * 48, 48), :] = (half[b, r, :] + own[slot, r, :]).astype(BF16)
            return 0

        lax.fori_loop(0, 2, far, 0)
        send(c1.at[b, 0:48], d1.at[0, b], pairsem(s_c1, 0, b), yup)
        send(c1.at[b, 48:96], d1.at[1, b], pairsem(s_c1, 1, b), ydn)

        def add(i, _):
            r = rows(i * 48, 48)
            half[b, r, :] = half[b, r, :] + own[slot, r, :]
            return 0

        lax.fori_loop(0, 8, add, 0)

    def stage_r(b):
        landed(d1.at[0, b], pairsem(s_c1, 0, b))
        c2[0, b, 0:48, :] = (half[b, rows(r_up, 48), :] + d1[0, b].astype(F32)).astype(BF16)
        c2[0, b, 48:96, :] = half[b, rows(r_up + 48, 48), :].astype(BF16)
        send(c2.at[0, b], e2.at[0, b], pairsem(s_c2, 0, b), yup)
        landed(d1.at[1, b], pairsem(s_c1, 1, b))
        c2[1, b, 0:48, :] = half[b, rows(r_dn, 48), :].astype(BF16)
        c2[1, b, 48:96, :] = (half[b, rows(r_dn + 48, 48), :] + d1[1, b].astype(F32)).astype(BF16)
        send(c2.at[1, b], e2.at[1, b], pairsem(s_c2, 1, b), ydn)

    def stage_t(b):
        landed(e2.at[0, b], pairsem(s_c2, 0, b))
        landed(e2.at[1, b], pairsem(s_c2, 1, b))

        def total(i, _):
            r = rows(r_own + i * 48, 48)
            q = rows(i * 48, 48)
            half[b, r, :] = half[b, r, :] + (e2[0, b, q, :].astype(F32) + e2[1, b, q, :].astype(F32))
            return 0

        lax.fori_loop(0, 2, total, 0)
        send(half.at[b, rows(r_own + 48 * (1 - xh), 48)], f2.at[b], pairsem(s_f, b), xpart)

    def block(index):
        return (chip * 2 + SLAB_SHIFT[index] + 16) % 16

    def spot(yy, xx):
        return rows(base + ((yy + 4) % 4) * 96 + xx * 48, 48)

    def send_spot(b, where, sem, device):
        send(amp.at[b, where], amp.at[b, where], sem, device)

    def stage_u(b):
        here = spot(y, xh)
        if b < N_PAIR:
            landed(f2.at[b], pairsem(s_f, b))
            left, right = PAIRS[b]
            value = half[b, rows(r_own + 48 * xh, 48), :] + f2[b]
            first = base + r_own + 48 * xh
            within = first % 256
            e_row = block(left) * 3 + first // 256
            e_next = block(left) * 3 + jnp.minimum(first // 256 + 1, 2)
            step = lax.broadcasted_iota(jnp.int32, (48, 128), 0) + within
            row_e = vcol[rows(within, 48), :] - jnp.where(step < 256, occ_e[e_row], occ_e[e_next])
            row_e = jnp.concatenate([row_e, row_e], axis=1)
            for j in range(3):
                col_e = virt[...] - occ_e[block(right) * 3 + j]
                cols = slice(j * 256, j * 256 + 256)
                amp[b, here, cols] = (value[:, cols] / (row_e + col_e)).astype(BF16)
            if b == 7:
                send(amp.at[7, here], amp.at[8, here], pairsem(s_z8), below)
        else:
            landed(amp.at[8, here], pairsem(s_z8))
        send_spot(b, here, pairsem(s_ax, b), xpart)
        send_spot(b, here, pairsem(s_ay, 0, xh, b), yup)
        send_spot(b, here, pairsem(s_ay, 1, xh, b), ydn)

    def stage_v(b):
        there = spot(y, 1 - xh)
        landed(amp.at[b, there], pairsem(s_ax, b))
        send_spot(b, there, pairsem(s_ay, 0, 1 - xh, b), yup)
        send_spot(b, there, pairsem(s_ay, 1, 1 - xh, b), ydn)

    def stage_w(b):
        landed(amp.at[b, spot(y - 1, 0)], pairsem(s_ay, 0, 0, b))
        send_spot(b, spot(y - 1, 0), pairsem(s_fw, 0, b), yup)
        landed(amp.at[b, spot(y + 1, 1)], pairsem(s_ay, 1, 1, b))
        send_spot(b, spot(y + 1, 1), pairsem(s_fw, 1, b), ydn)

    def stage_y(b):
        landed(amp.at[b, spot(y - 1, 1)], pairsem(s_ay, 0, 1, b))
        landed(amp.at[b, spot(y + 1, 0)], pairsem(s_ay, 1, 0, b))
        landed(amp.at[b, spot(y + 2, 0)], pairsem(s_fw, 0, b))
        landed(amp.at[b, spot(y + 2, 1)], pairsem(s_fw, 1, b))
        part = rows(base, 384)
        send(amp.at[b, part], amp.at[b, part], pairsem(s_sib, b), sibling)

    def plain(b, s, k):
        return jnp.dot(amp[b, rows(k * 256, 256), :], slab[s], preferred_element_type=F32)

    def turned(b, s, k):
        return lax.dot_general(
            amp[b, :, pl.ds(pl.multiple_of(k * 256, 256), 256)], slab[s],
            (((0,), (0,)), ((), ())), preferred_element_type=F32)

    def accumulate(which, terms, first):
        def piece(k, _):
            r = rows(k * 256, 256)
            value = None if first else gam[which, r, :]
            for kind, b, s in terms:
                term = kind(b, s, k)
                value = term if value is None else value + term
            gam[which, r, :] = value
            return 0
        lax.fori_loop(0, 3, piece, 0)

    def hand_back(way, terms, device):
        for k in range(3):
            value = None
            for kind, b, s in terms:
                term = kind(b, s, k)
                value = term if value is None else value + term
            bsend[way, k * 256:(k + 1) * 256, :] = value.astype(BF16)
            part = slice(k * 256, (k + 1) * 256)
            send(bsend.at[way, part], brecv.at[way, part], pairsem(s_back, way, k), device)

    complete = set()

    def stage_z(b):
        away = rows(384 - base, 384)
        landed(amp.at[b, away], pairsem(s_sib, b))
        complete.add(b)
        if b == 6 or b == 5:
            if 5 in complete and 6 in complete:
                hand_back(0, [(plain, 5, 0), (plain, 6, 2)], above)
        if b in (3, 4, 6) and {3, 4, 6} <= complete:
            hand_back(1, [(turned, 3, 0), (turned, 4, 1), (turned, 6, 4)], below)
        if b < 3 and {0, 1, 2} <= complete:
            accumulate(0, [(plain, 0, 0), (turned, 2, 1)], True)
            accumulate(1, [(plain, 2, 0), (plain, 1, 1)], True)

    stages = dict(P=stage_p, Q=stage_q, R=stage_r, T=stage_t, U=stage_u, V=stage_v, W=stage_w,
                  Y=stage_y, Z=stage_z)
    for stage, b in schedule():
        stages[stage](b)
    need(5)
    accumulate(0, [(plain, 3, 2), (turned, 5, 4), (turned, 8, 5)], False)
    accumulate(1, [(plain, 4, 2), (plain, 7, 3)], False)

    locals_ = []
    for k in range(3):
        part = slice(k * 256, (k + 1) * 256)
        for way in range(2):
            landed(brecv.at[way, part], pairsem(s_back, way, k))
            gam[way, part, :] = gam[way, part, :] + brecv[way, part, :].astype(F32)
        send(gam.at[1 - core, part], out.at[part, mine], pairsem(s_out, k), sibling)
        copy = pltpu.make_async_copy(gam.at[core, part], out.at[part, mine], s_out.at[2, k])
        copy.start()
        locals_.append(copy)
    for k in range(3):
        landed(out.at[k * 256:(k + 1) * 256, other], pairsem(s_out, k))
    for copy in locals_:
        copy.wait()
    for copy in pending + list(gives.values()):
        copy.wait_send()


def per_device(orbital_b, block_size, occ_energy, virt_energy):
    block = orbital_b.reshape(768, 1536)
    dma = pltpu.SemaphoreType.DMA
    vmem = pltpu.VMEM
    result = pl.pallas_call(
        kernel,
        out_shape=jax.ShapeDtypeStruct((768, 1536), F32),
        in_specs=[
            pl.BlockSpec(memory_space=pltpu.VMEM),
            pl.BlockSpec(memory_space=pltpu.SMEM),
            pl.BlockSpec(memory_space=pltpu.SMEM),
            pl.BlockSpec(memory_space=pltpu.VMEM),
        ],
        out_specs=pl.BlockSpec(memory_space=pl.ANY),
        scratch_shapes=[
            vmem((768, 768), BF16),
            vmem((6, 768, 768), BF16),
            vmem((3, 384, 768), F32),
            vmem((3, 384, 768), F32),
            vmem((N_PAIR, 384, 768), F32),
            vmem((N_PAIR, 96, 768), BF16),
            vmem((2, N_PAIR, 48, 768), BF16),
            vmem((2, N_PAIR, 96, 768), BF16),
            vmem((2, N_PAIR, 96, 768), BF16),
            vmem((N_PAIR, 48, 768), F32),
            vmem((N_PAIR + 1, 768, 768), BF16),
            vmem((2, 768, 768), F32),
            vmem((2, 768, 768), BF16),
            vmem((2, 768, 768), BF16),
            vmem((512, 128), F32),
            dma((2,)),
            dma((2, 4)),
            dma((2, N_PAIR)),
            dma((2, 2, N_PAIR)),
            dma((2, 2, N_PAIR)),
            dma((2, N_PAIR)),
            dma((2, N_PAIR + 1)),
            dma((2, 2, 2, N_PAIR + 1)),
            dma((2, 2, N_PAIR + 1)),
            dma((2, N_PAIR + 1)),
            dma((2,)),
            dma((2, 2, 3)),
            dma((3, 3)),
        ],
        compiler_params=pltpu.CompilerParams(
            collective_id=0, has_side_effects=True, vmem_limit_bytes=62 * 2**20),
        name="window_gamma",
    )(block, block_size, occ_energy, virt_energy.reshape(1, 256))
    return result.reshape(3, 256, 1536)


def solution(mesh):
    in_specs = (P("occ", None, "aux"), P(), P(), P())
    out_specs = P("occ", None, "aux")
    return jax.shard_map(
        per_device, mesh=mesh, in_specs=in_specs, out_specs=out_specs, check_vma=False
    )
```

time: 604 us -> 195 us (0.32)
  the two profiles are of different devices: /device:TPU:96 before, /device:TPU:1 now
where the time goes in v1:
time: 195 us
  Pallas kernels  190 us (97%)
  local copies, waits for them, and re-layouts  4.84 us (2%)
    pallas_call x1, Pallas kernels, per_device(): pl.pallas_call(kernel, out_shape=jax.ShapeDtypeStruct((768, 1536), F32),...  190 us
    unnamed x1, local copies, waits for them, and re-layouts  4.84 us

profile of v1, /device:TPU:1, one launch (start us, length us, event | category | flops | bytes accessed | tf_op | source)
XLA Modules:
  0.0 195.0 jit_solution(3623911961083184665)
XLA Ops:
  0.0 190.2 %window_gamma.1 = f32[768,1536]{1,0:T(8,128)} custom-call(bf16[768,1536]{1,0:T(8,128)(2,1)} %bitcast.4, s32[16]{0:T(128)} %sizes.1, f32[48]{0:T(128)} %occ_e.1, f32[1,256]{1,0:T(1,128)} %bitcast.5), custom_call_target="tpu_custom_call" | custom-call | tf_op jit(solution)/shard_map/window_gamma/pallas_call | solution.py:314
  190.2 4.8 %copy.6 = f32[3,256,1536]{2,1,0:T(8,128)} copy(f32[3,256,1536]{2,1,0:T(8,128)} %bitcast.3) | data formatting | bytes 9437184

commit v2 on v1

v2 whole, which is shorter than its diff:
```python
import jax
import jax.numpy as jnp
from jax import lax
from jax.experimental import pallas as pl
from jax.experimental.pallas import tpu as pltpu
from jax.sharding import PartitionSpec as P

MESH = pl.DeviceIdType.MESH
BF16 = jnp.bfloat16
F32 = jnp.float32

SLAB_SHIFT = (0, 1, -1, -2, 2, 3)
BATCHES = (
    tuple((0, 0, k) for k in range(3)),
    tuple((1, 1, k) for k in range(3)),
    tuple((1, 0, k) for k in range(3)),
    ((0, 2, 0), (1, 2, 0), (0, 4, 0)),
    ((0, 2, 1), (1, 2, 1), (0, 4, 1)),
    ((0, 2, 2), (1, 2, 2), (0, 4, 2)),
    tuple((4, 2, k) for k in range(3)),
    tuple((1, 3, k) for k in range(3)),
)
N_PAIR = len(BATCHES)
AHEAD = 2

ORDER = (
    ("P", 2), ("P", 1), ("N", 0), ("Q", 2), ("Q", 1), ("P", 0), ("N", 1), ("R", 2), ("P", 3), ("N", 2),
    ("T", 2), ("Q", 3), ("R", 1), ("Q", 0), ("N", 3), ("R", 3), ("P", 4), ("N", 4), ("T", 1), ("Q", 4),
    ("R", 0), ("U", 2), ("N", 5), ("P", 6), ("N", 6), ("Q", 6), ("W", 2), ("T", 3), ("R", 6), ("Y", 2),
    ("N", 7), ("U", 1), ("Z", 2), ("R", 4), ("T", 6), ("N", 8), ("P", 5), ("W", 1), ("Q", 5), ("U", 3),
    ("N", 9), ("Y", 1), ("T", 4), ("Z", 1), ("T", 0), ("R", 5), ("U", 6), ("W", 3), ("T", 5), ("P", 7),
    ("W", 6), ("Q", 7), ("Y", 6), ("Y", 3), ("U", 4), ("R", 7), ("Z", 6), ("Z", 3), ("B", 0), ("W", 4),
    ("U", 0), ("U", 5), ("T", 7), ("Y", 4), ("Z", 4), ("B", 1), ("W", 0), ("W", 5), ("U", 7), ("Y", 0),
    ("Z", 0), ("Y", 5), ("A", 0), ("W", 7), ("U", 8), ("Y", 7), ("Z", 5), ("B", 2), ("Z", 7), ("W", 8),
    ("C", 0), ("Y", 8), ("Z", 8),
)


def rows(start, size, align=16):
    return pl.ds(pl.multiple_of(start, align), size)


def kernel(orb, sizes, occ_e, virt, out, back, swap, slab, own, give, half, c1, d1, c2, e2, f1, f2,
           amp, gam, bsend, vcol, s_swap, s_slab, s_half, s_c1, s_c2, s_f, s_ay, s_fw,
           s_sib, s_z8, s_back, s_out):
    o = lax.axis_index("occ")
    a = lax.axis_index("aux")
    chip, core = o // 2, o % 2
    xh, y = a // 4, a % 4
    sibling = (chip * 2 + 1 - core, a)
    up2 = ((chip + 1) % 8) * 2
    dn2 = ((chip + 7) % 8) * 2
    below = (dn2 + core, a)
    yup = (o, xh * 4 + (y + 1) % 4)
    ydn = (o, xh * 4 + (y + 3) % 4)
    xpart = (o, (1 - xh) * 4 + y)
    partners = (sibling, yup, ydn, xpart, (up2, a), (up2 + 1, a), (dn2, a), (dn2 + 1, a))

    barrier = pltpu.get_barrier_semaphore()
    for device in partners:
        pl.semaphore_signal(barrier, inc=1, device_id=device, device_id_type=MESH)
    pending = []

    def remote(src, dst, sems, device):
        copy = pltpu.make_async_remote_copy(
            src_ref=src, dst_ref=dst, send_sem=sems[0], recv_sem=sems[1], device_id=device,
            device_id_type=MESH)
        return copy

    def send(src, dst, sems, device):
        copy = remote(src, dst, sems, device)
        copy.start()
        pending.append(copy)
        return copy

    def landed(dst, sems):
        remote(dst, dst, sems, sibling).wait_recv()

    def pairsem(sem, *index):
        return sem.at[(0,) + index], sem.at[(1,) + index]

    mine = pl.ds(pl.multiple_of(core * 768, 128), 768)
    other = pl.ds(pl.multiple_of((1 - core) * 768, 128), 768)
    live = sizes[o]

    def mask_other(i, _):
        r = rows(i * 64, 64)
        swap[r, :] = jnp.where(i // 4 < live, orb[r, other], jnp.zeros((64, 768), BF16))
        return 0

    def mask_mine(i, _):
        r = rows(i * 64, 64)
        slab[core, r, :] = jnp.where(i // 4 < live, orb[r, mine], jnp.zeros((64, 768), BF16))
        return 0

    lax.fori_loop(0, 12, mask_other, 0)
    lax.fori_loop(0, 12, mask_mine, 0)
    pl.semaphore_wait(barrier, len(partners))

    def send_chunk(i):
        part = slice(i % 6 * 128, i % 6 * 128 + 128)
        for d, (which, index, chip2) in enumerate((
                (1 - i // 6, 2 + i // 6, up2), (i // 6, 4 + i // 6, dn2))):
            chunk = remote(slab.at[which, part], slab.at[index, part], pairsem(s_slab, d, i), (chip2 + core, a))
            chunk.start()
            chunks[d, i] = chunk

    chunks = {}
    send(swap.at[0:256], slab.at[core, 0:256], pairsem(s_swap, 0), sibling)
    send(swap.at[256:768], slab.at[core, 256:768], pairsem(s_swap, 1), sibling)
    landed(slab.at[1 - core, 0:256], pairsem(s_swap, 0))
    for i in range(AHEAD):
        send_chunk(i)

    column = jnp.broadcast_to(virt[...], (128, 256)).T
    vcol[0:256, :] = column
    vcol[256:512, :] = column

    landed(slab.at[1 - core, 256:768], pairsem(s_swap, 1))
    arrived = set()

    def need(index, k):
        if index < 2 or (index, k) in arrived:
            return
        d, late = (index - 2) // 2, index % 2 * 6
        for i in (2 * k, 2 * k + 1):
            landed(slab.at[index, i * 128:i * 128 + 128], pairsem(s_slab, d, late + i))
        arrived.add((index, k))

    def stage_n(i):
        for d in range(2):
            chunks[d, i].wait_send()
        send_chunk(i + AHEAD)

    base = core * 384
    r_own = y * 96
    r_up = ((y + 1) % 4) * 96
    r_dn = ((y + 3) % 4) * 96
    r_far = ((y + 2) % 4) * 96
    gives, taken = {}, {}

    def stage_p(b):
        for left, right, k in BATCHES[b]:
            need(right, k)
            for i in range(3):
                need(left, i)
        slot = taken[b] = min({0, 1, 2} - set(taken.values()))
        if slot in gives:
            gives[slot].wait_send()

        def product(dst, first):
            for j, (left, right, k) in enumerate(BATCHES[b]):
                dst[slot, :, j * 256:j * 256 + 256] = lax.dot_general(
                    slab[left, rows(first, 384), :], slab[right, k * 256:k * 256 + 256, :],
                    (((1,), (1,)), ((), ())), preferred_element_type=F32)

        product(give, 384 - base)
        gives[slot] = remote(give.at[slot], half.at[b], pairsem(s_half, b), sibling)
        gives[slot].start()
        product(own, base)

    def stage_q(b):
        slot = taken.pop(b)
        landed(half.at[b], pairsem(s_half, b))

        def far(i, _):
            r = rows(r_far + i * 48, 48)
            c1[b, rows(i * 48, 48), :] = (half[b, r, :] + own[slot, r, :]).astype(BF16)
            return 0

        lax.fori_loop(0, 2, far, 0)
        send(c1.at[b, 0:48], d1.at[0, b], pairsem(s_c1, 0, b), yup)
        send(c1.at[b, 48:96], d1.at[1, b], pairsem(s_c1, 1, b), ydn)

        def add(i, _):
            r = rows(i * 48, 48)
            half[b, r, :] = half[b, r, :] + own[slot, r, :]
            return 0

        lax.fori_loop(0, 8, add, 0)

    def stage_r(b):
        landed(d1.at[0, b], pairsem(s_c1, 0, b))
        c2[0, b, 0:48, :] = (half[b, rows(r_up, 48), :] + d1[0, b].astype(F32)).astype(BF16)
        c2[0, b, 48:96, :] = half[b, rows(r_up + 48, 48), :].astype(BF16)
        send(c2.at[0, b], e2.at[0, b], pairsem(s_c2, 0, b), yup)
        landed(d1.at[1, b], pairsem(s_c1, 1, b))
        c2[1, b, 0:48, :] = half[b, rows(r_dn, 48), :].astype(BF16)
        c2[1, b, 48:96, :] = (half[b, rows(r_dn + 48, 48), :] + d1[1, b].astype(F32)).astype(BF16)
        send(c2.at[1, b], e2.at[1, b], pairsem(s_c2, 1, b), ydn)

    def stage_t(b):
        landed(e2.at[0, b], pairsem(s_c2, 0, b))
        landed(e2.at[1, b], pairsem(s_c2, 1, b))

        def total(i, _):
            r = rows(r_own + i * 48, 48)
            q = rows(i * 48, 48)
            value = half[b, r, :] + (e2[0, b, q, :].astype(F32) + e2[1, b, q, :].astype(F32))
            half[b, r, :] = value
            f1[b, q, :] = value.astype(BF16)
            return 0

        lax.fori_loop(0, 2, total, 0)
        send(f1.at[b], f2.at[b], pairsem(s_f, b), xpart)

    def block(index):
        return (chip * 2 + SLAB_SHIFT[index] + 16) % 16

    def spot(yy):
        return rows(base + ((yy + 4) % 4) * 96, 96)

    def halfspot(yy, i):
        return rows(base + ((yy + 4) % 4) * 96 + i * 48, 48)

    def send_spot(b, where, sem, device):
        send(amp.at[b, where], amp.at[b, where], sem, device)

    def stage_u(b):
        here = spot(y)
        if b < N_PAIR:
            landed(f2.at[b], pairsem(s_f, b))
            first = base + r_own
            within = first % 256
            step = lax.broadcasted_iota(jnp.int32, (96, 128), 0) + within
            for j, (left, right, k) in enumerate(BATCHES[b]):
                e_row = block(left) * 3 + first // 256
                e_next = block(left) * 3 + jnp.minimum(first // 256 + 1, 2)
                row_e = vcol[rows(within, 96), :] - jnp.where(step < 256, occ_e[e_row], occ_e[e_next])
                row_e = jnp.concatenate([row_e, row_e], axis=1)
                col_e = virt[...] - occ_e[block(right) * 3 + k]
                lanes = slice(j * 256, j * 256 + 256)
                value = half[b, rows(r_own, 96), lanes] + f2[b, :, lanes].astype(F32)
                amp[b, here, lanes] = (value / (row_e + col_e)).astype(BF16)
            if b == 7:
                send(amp.at[7, here], amp.at[8, here], pairsem(s_z8), below)
        else:
            landed(amp.at[8, here], pairsem(s_z8))
        send_spot(b, here, pairsem(s_ay, 0, b), yup)
        send_spot(b, here, pairsem(s_ay, 1, b), ydn)

    def stage_w(b):
        landed(amp.at[b, spot(y - 1)], pairsem(s_ay, 0, b))
        send_spot(b, halfspot(y - 1, 0), pairsem(s_fw, 0, b), yup)
        landed(amp.at[b, spot(y + 1)], pairsem(s_ay, 1, b))
        send_spot(b, halfspot(y + 1, 1), pairsem(s_fw, 1, b), ydn)

    def stage_y(b):
        landed(amp.at[b, halfspot(y + 2, 0)], pairsem(s_fw, 0, b))
        landed(amp.at[b, halfspot(y + 2, 1)], pairsem(s_fw, 1, b))
        part = rows(base, 384)
        send(amp.at[b, part], amp.at[b, part], pairsem(s_sib, b), sibling)

    def cols(k):
        return slice(k * 256, k * 256 + 256)

    def plain(b, s):
        return lambda k: jnp.dot(amp[b, cols(k), :], slab[s], preferred_element_type=F32)

    def turned(b, s):
        return lambda k: lax.dot_general(
            amp[b, :, cols(k)], slab[s], (((0,), (0,)), ((), ())), preferred_element_type=F32)

    def turned_unit(j, s):
        return lambda k: lax.dot_general(
            amp[3 + k, :, cols(j)], slab[s], (((0,), (0,)), ((), ())), preferred_element_type=F32)

    def units(j, s):
        def term(k):
            value = None
            for i in range(3):
                part = jnp.dot(amp[3 + i, cols(k), cols(j)], slab[s, cols(i), :], preferred_element_type=F32)
                value = part if value is None else value + part
            return value
        return term

    def total_of(terms, k):
        value = terms[0](k)
        for term in terms[1:]:
            value = value + term(k)
        return value

    def accumulate(which, terms, first):
        for k in range(3):
            value = total_of(terms, k)
            gam[which, cols(k), :] = value if first else gam[which, cols(k), :] + value

    def hand_back(k):
        bsend[0, cols(k), :] = total_of(
            [turned_unit(0, 0), turned_unit(1, 1), turned(6, 4)], k).astype(BF16)
        send(bsend.at[0, cols(k)], back.at[cols(k), mine],
             (s_back.at[0, 0, k], s_back.at[1, core, k]), (dn2 + 1, a))
        bsend[1, cols(k), :] = total_of([turned_unit(2, 0), plain(6, 2)], k).astype(BF16)
        send(bsend.at[1, cols(k)], back.at[cols(k), mine],
             (s_back.at[0, 1, k], s_back.at[1, core, k]), (up2, a))

    def stage_z(b):
        landed(amp.at[b, rows(384 - base, 384)], pairsem(s_sib, b))

    def stage_a(_):
        accumulate(0, [plain(0, 0), turned(2, 1)], True)
        accumulate(1, [plain(2, 0), plain(1, 1)], True)

    def stage_c(_):
        accumulate(0, [units(0, 2), units(2, 4)], False)
        accumulate(1, [units(1, 2)], False)

    stages = dict(P=stage_p, Q=stage_q, R=stage_r, T=stage_t, U=stage_u, W=stage_w, Y=stage_y, Z=stage_z,
                  N=stage_n, B=hand_back, A=stage_a, C=stage_c)
    for stage, b in ORDER:
        stages[stage](b)
    for k in range(3):
        need(5, k)
    locals_ = []
    for k in range(3):
        for which, terms in ((0, [turned(8, 5)]), (1, [plain(7, 3)])):
            gam[which, cols(k), :] = gam[which, cols(k), :] + total_of(terms, k)
        send(gam.at[1 - core, cols(k)], out.at[cols(k), mine], pairsem(s_out, k), sibling)
        copy = pltpu.make_async_copy(gam.at[core, cols(k)], out.at[cols(k), mine], s_out.at[2, k])
        copy.start()
        locals_.append(copy)
    for k in range(3):
        landed(out.at[cols(k), other], pairsem(s_out, k))
        for j in range(2):
            landed(back.at[cols(k), j * 768:j * 768 + 768], (s_back.at[0, 0, k], s_back.at[1, j, k]))
    for copy in locals_:
        copy.wait()
    for i in range(12 - AHEAD, 12):
        for d in range(2):
            chunks[d, i].wait_send()
    for copy in pending + list(gives.values()):
        copy.wait_send()


def per_device(orbital_b, block_size, occ_energy, virt_energy):
    block = orbital_b.reshape(768, 1536)
    dma = pltpu.SemaphoreType.DMA
    vmem = pltpu.VMEM
    partial, shares = pl.pallas_call(
        kernel,
        out_shape=(jax.ShapeDtypeStruct((768, 1536), F32), jax.ShapeDtypeStruct((768, 1536), BF16)),
        in_specs=[
            pl.BlockSpec(memory_space=pltpu.VMEM),
            pl.BlockSpec(memory_space=pltpu.SMEM),
            pl.BlockSpec(memory_space=pltpu.SMEM),
            pl.BlockSpec(memory_space=pltpu.VMEM),
        ],
        out_specs=(pl.BlockSpec(memory_space=pl.ANY), pl.BlockSpec(memory_space=pl.ANY)),
        scratch_shapes=[
            vmem((768, 768), BF16),
            vmem((6, 768, 768), BF16),
            vmem((3, 384, 768), F32),
            vmem((3, 384, 768), F32),
            vmem((N_PAIR, 384, 768), F32),
            vmem((N_PAIR, 96, 768), BF16),
            vmem((2, N_PAIR, 48, 768), BF16),
            vmem((2, N_PAIR, 96, 768), BF16),
            vmem((2, N_PAIR, 96, 768), BF16),
            vmem((N_PAIR, 96, 768), BF16),
            vmem((N_PAIR, 96, 768), BF16),
            vmem((N_PAIR + 1, 768, 768), BF16),
            vmem((2, 768, 768), F32),
            vmem((2, 768, 768), BF16),
            vmem((512, 128), F32),
            dma((2, 2)),
            dma((2, 2, 12)),
            dma((2, N_PAIR)),
            dma((2, 2, N_PAIR)),
            dma((2, 2, N_PAIR)),
            dma((2, N_PAIR)),
            dma((2, 2, N_PAIR + 1)),
            dma((2, 2, N_PAIR + 1)),
            dma((2, N_PAIR + 1)),
            dma((2,)),
            dma((2, 2, 3)),
            dma((3, 3)),
        ],
        compiler_params=pltpu.CompilerParams(
            collective_id=0, has_side_effects=True, vmem_limit_bytes=62 * 2**20),
        name="window_gamma",
    )(block, block_size, occ_energy, virt_energy.reshape(1, 256))
    return (partial + shares.astype(F32)).reshape(3, 256, 1536)


def solution(mesh):
    in_specs = (P("occ", None, "aux"), P(), P(), P())
    out_specs = P("occ", None, "aux")
    return jax.shard_map(
        per_device, mesh=mesh, in_specs=in_specs, out_specs=out_specs, check_vma=False
    )
```

time: 195 us -> 135 us (0.69)
  Pallas kernels: 190 us -> 129 us
  other arithmetic: 0 us -> 5.99 us
  local copies, waits for them, and re-layouts: 4.84 us -> 0 us
    pallas_call x1, Pallas kernels: 190 us -> 129 us  [per_device(): pl.pallas_call(kernel, out_shape=(jax.ShapeDtypeStruct((768, 1536), F32),...]
    add x0 -> x1, other arithmetic: none -> 5.99 us  [per_device(): return (partial + shares.astype(F32)).reshape(3, 256, 1536)]
    unnamed x1 -> x0, local copies, waits for them, and re-layouts: 4.84 us -> none
where the time goes in v2:
time: 135 us
  Pallas kernels  129 us (96%)
  other arithmetic  5.99 us (4%)
    pallas_call x1, Pallas kernels, per_device(): pl.pallas_call(kernel, out_shape=(jax.ShapeDtypeStruct((768, 1536), F32),...  129 us
    add x1, other arithmetic, per_device(): return (partial + shares.astype(F32)).reshape(3, 256, 1536)  5.99 us

profile of v2, /device:TPU:1, one launch (start us, length us, event | category | flops | bytes accessed | tf_op | source)
XLA Modules:
  0.0 135.0 jit_solution(5146385148641843064)
XLA Ops:
  0.0 129.0 %window_gamma.1 = (f32[768,1536]{1,0:T(8,128)}, bf16[768,1536]{1,0:T(8,128)(2,1)}) custom-call(bf16[768,1536]{1,0:T(8,128)(2,1)} %bitcast.3, s32[16]{0:T(128)} %sizes.1, f32[48]{0:T(128)} %occ_e.1, f32[1,256]{1,0:T(1,128)} %bitcast.4), custom_call_target="tpu_custom_call" | custom-call | tf_op jit(solution)/shard_map/window_gamma/pallas_call | solution.py:339
  129.0 6.0 %convert_add_fusion = f32[768,1536]{1,0:T(8,128)} fusion(f32[768,1536]{1,0:T(8,128)} %get-tuple-element.7, bf16[768,1536]{1,0:T(8,128)(2,1)} %get-tuple-element.8), kind=kLoop, calls=%fused_computation | loop fusion | flops 2359296 | bytes 11796480 | tf_op jit(solution)/shard_map/add | solution.py:382

commit v3 on v2

--- a/solution.py
+++ b/solution.py
@@ -10,9 +10,10 @@
 F32 = jnp.float32
 
 SLAB_SHIFT = (0, 1, -1, -2, 2, 3)
+PACKED = 3
 BATCHES = (
-    tuple((0, 0, k) for k in range(3)),
-    tuple((1, 1, k) for k in range(3)),
+    ((0, 0, 0), (0, 0, PACKED)),
+    ((1, 1, 0), (1, 1, PACKED)),
     tuple((1, 0, k) for k in range(3)),
     ((0, 2, 0), (1, 2, 0), (0, 4, 0)),
     ((0, 2, 1), (1, 2, 1), (0, 4, 1)),
@@ -24,15 +25,15 @@
 AHEAD = 2
 
 ORDER = (
-    ("P", 2), ("P", 1), ("N", 0), ("Q", 2), ("Q", 1), ("P", 0), ("N", 1), ("R", 2), ("P", 3), ("N", 2),
-    ("T", 2), ("Q", 3), ("R", 1), ("Q", 0), ("N", 3), ("R", 3), ("P", 4), ("N", 4), ("T", 1), ("Q", 4),
-    ("R", 0), ("U", 2), ("N", 5), ("P", 6), ("N", 6), ("Q", 6), ("W", 2), ("T", 3), ("R", 6), ("Y", 2),
-    ("N", 7), ("U", 1), ("Z", 2), ("R", 4), ("T", 6), ("N", 8), ("P", 5), ("W", 1), ("Q", 5), ("U", 3),
-    ("N", 9), ("Y", 1), ("T", 4), ("Z", 1), ("T", 0), ("R", 5), ("U", 6), ("W", 3), ("T", 5), ("P", 7),
-    ("W", 6), ("Q", 7), ("Y", 6), ("Y", 3), ("U", 4), ("R", 7), ("Z", 6), ("Z", 3), ("B", 0), ("W", 4),
-    ("U", 0), ("U", 5), ("T", 7), ("Y", 4), ("Z", 4), ("B", 1), ("W", 0), ("W", 5), ("U", 7), ("Y", 0),
-    ("Z", 0), ("Y", 5), ("A", 0), ("W", 7), ("U", 8), ("Y", 7), ("Z", 5), ("B", 2), ("Z", 7), ("W", 8),
-    ("C", 0), ("Y", 8), ("Z", 8),
+    ("P", 0), ("P", 2), ("P", 1), ("Q", 0), ("Q", 2), ("N", 0), ("Q", 1), ("R", 2), ("N", 1), ("P", 3),
+    ("N", 2), ("Q", 3), ("R", 3), ("R", 0), ("N", 3), ("P", 4), ("N", 4), ("T", 3), ("Q", 4), ("R", 1),
+    ("R", 4), ("N", 5), ("T", 0), ("P", 5), ("P", 6), ("N", 6), ("Q", 6), ("R", 6), ("U", 3), ("N", 7),
+    ("Q", 5), ("U", 0), ("T", 6), ("N", 8), ("W", 3), ("R", 5), ("T", 2), ("N", 9), ("W", 0), ("Y", 3),
+    ("Z", 3), ("U", 6), ("T", 5), ("T", 4), ("T", 1), ("Y", 0), ("Z", 0), ("W", 6), ("U", 2), ("P", 7),
+    ("Y", 6), ("Q", 7), ("Z", 6), ("U", 5), ("B", 0), ("R", 7), ("U", 4), ("U", 1), ("W", 5), ("T", 7),
+    ("W", 4), ("W", 2), ("W", 1), ("Y", 5), ("U", 7), ("Z", 5), ("Y", 4), ("B", 2), ("Y", 2), ("Z", 4),
+    ("B", 1), ("Y", 1), ("Z", 2), ("U", 8), ("W", 7), ("Z", 1), ("A", 1), ("A", 0), ("W", 8), ("C", 0),
+    ("Y", 7), ("C", 1), ("Y", 8), ("Z", 7), ("D", 7), ("Z", 8), ("D", 8),
 )
 
 
@@ -40,9 +41,9 @@
     return pl.ds(pl.multiple_of(start, align), size)
 
 
-def kernel(orb, sizes, occ_e, virt, out, back, swap, slab, own, give, half, c1, d1, c2, e2, f1, f2,
+def kernel(orb_hbm, sizes, occ_e, virt, out, back, orb, swap, slab, own, give, half, c1, d1, c2, e2, f1, f2,
            amp, gam, bsend, vcol, s_swap, s_slab, s_half, s_c1, s_c2, s_f, s_ay, s_fw,
-           s_sib, s_z8, s_back, s_out):
+           s_sib, s_z8, s_back, s_out, s_load):
     o = lax.axis_index("occ")
     a = lax.axis_index("aux")
     chip, core = o // 2, o % 2
@@ -56,6 +57,8 @@
     xpart = (o, (1 - xh) * 4 + y)
     partners = (sibling, yup, ydn, xpart, (up2, a), (up2 + 1, a), (dn2, a), (dn2 + 1, a))
 
+    load = pltpu.make_async_copy(orb_hbm, orb, s_load)
+    load.start()
     barrier = pltpu.get_barrier_semaphore()
     for device in partners:
         pl.semaphore_signal(barrier, inc=1, device_id=device, device_id_type=MESH)
@@ -93,6 +96,7 @@
         slab[core, r, :] = jnp.where(i // 4 < live, orb[r, mine], jnp.zeros((64, 768), BF16))
         return 0
 
+    load.wait()
     lax.fori_loop(0, 12, mask_other, 0)
     lax.fori_loop(0, 12, mask_mine, 0)
     pl.semaphore_wait(barrier, len(partners))
@@ -148,61 +152,76 @@
         if slot in gives:
             gives[slot].wait_send()
 
-        def product(dst, first):
+        def product(dst, side):
             for j, (left, right, k) in enumerate(BATCHES[b]):
-                dst[slot, :, j * 256:j * 256 + 256] = lax.dot_general(
-                    slab[left, rows(first, 384), :], slab[right, k * 256:k * 256 + 256, :],
-                    (((1,), (1,)), ((), ())), preferred_element_type=F32)
-
-        product(give, 384 - base)
-        gives[slot] = remote(give.at[slot], half.at[b], pairsem(s_half, b), sibling)
+                lanes = slice(j * 256, j * 256 + 256)
+                if k == PACKED:
+                    for p in range(3):
+                        row = 256 + 128 * p + side * (384, 128, 128)[p]
+                        col = 256 + side * (0, 256, 256)[p]
+                        dst[slot, p * 128:p * 128 + 128, lanes] = lax.dot_general(
+                            slab[left, rows(row, 128), :], slab[right, rows(col, 256), :],
+                            (((1,), (1,)), ((), ())), preferred_element_type=F32)
+                else:
+                    dst[slot, :, lanes] = lax.dot_general(
+                        slab[left, rows(side * 384, 384), :], slab[right, k * 256:k * 256 + 256, :],
+                        (((1,), (1,)), ((), ())), preferred_element_type=F32)
+
+        w = wide(b)
+        product(give, 1 - core)
+        gives[slot] = remote(give.at[slot, :, w], half.at[b, :, w], pairsem(s_half, b), sibling)
         gives[slot].start()
-        product(own, base)
+        product(own, core)
+
+    def wide(b):
+        return slice(0, 256 * len(BATCHES[min(b, 7)]))
 
     def stage_q(b):
-        slot = taken.pop(b)
-        landed(half.at[b], pairsem(s_half, b))
+        slot, w = taken.pop(b), wide(b)
+        landed(half.at[b, :, w], pairsem(s_half, b))
 
         def far(i, _):
             r = rows(r_far + i * 48, 48)
-            c1[b, rows(i * 48, 48), :] = (half[b, r, :] + own[slot, r, :]).astype(BF16)
+            c1[b, rows(i * 48, 48), w] = (half[b, r, w] + own[slot, r, w]).astype(BF16)
             return 0
 
         lax.fori_loop(0, 2, far, 0)
-        send(c1.at[b, 0:48], d1.at[0, b], pairsem(s_c1, 0, b), yup)
-        send(c1.at[b, 48:96], d1.at[1, b], pairsem(s_c1, 1, b), ydn)
+        send(c1.at[b, 0:48, w], d1.at[0, b, :, w], pairsem(s_c1, 0, b), yup)
+        send(c1.at[b, 48:96, w], d1.at[1, b, :, w], pairsem(s_c1, 1, b), ydn)
 
         def add(i, _):
             r = rows(i * 48, 48)
-            half[b, r, :] = half[b, r, :] + own[slot, r, :]
+            half[b, r, w] = half[b, r, w] + own[slot, r, w]
             return 0
 
         lax.fori_loop(0, 8, add, 0)
 
     def stage_r(b):
-        landed(d1.at[0, b], pairsem(s_c1, 0, b))
-        c2[0, b, 0:48, :] = (half[b, rows(r_up, 48), :] + d1[0, b].astype(F32)).astype(BF16)
-        c2[0, b, 48:96, :] = half[b, rows(r_up + 48, 48), :].astype(BF16)
-        send(c2.at[0, b], e2.at[0, b], pairsem(s_c2, 0, b), yup)
-        landed(d1.at[1, b], pairsem(s_c1, 1, b))
-        c2[1, b, 0:48, :] = half[b, rows(r_dn, 48), :].astype(BF16)
-        c2[1, b, 48:96, :] = (half[b, rows(r_dn + 48, 48), :] + d1[1, b].astype(F32)).astype(BF16)
-        send(c2.at[1, b], e2.at[1, b], pairsem(s_c2, 1, b), ydn)
+        w = wide(b)
+        landed(d1.at[0, b, :, w], pairsem(s_c1, 0, b))
+        c2[0, b, 0:48, w] = (half[b, rows(r_up, 48), w] + d1[0, b, :, w].astype(F32)).astype(BF16)
+        c2[0, b, 48:96, w] = half[b, rows(r_up + 48, 48), w].astype(BF16)
+        send(c2.at[0, b, :, w], e2.at[0, b, :, w], pairsem(s_c2, 0, b), yup)
+        landed(d1.at[1, b, :, w], pairsem(s_c1, 1, b))
+        c2[1, b, 0:48, w] = half[b, rows(r_dn, 48), w].astype(BF16)
+        c2[1, b, 48:96, w] = (half[b, rows(r_dn + 48, 48), w] + d1[1, b, :, w].astype(F32)).astype(BF16)
+        send(c2.at[1, b, :, w], e2.at[1, b, :, w], pairsem(s_c2, 1, b), ydn)
 
     def stage_t(b):
-        landed(e2.at[0, b], pairsem(s_c2, 0, b))
-        landed(e2.at[1, b], pairsem(s_c2, 1, b))
+        w = wide(b)
+        landed(e2.at[0, b, :, w], pairsem(s_c2, 0, b))
+        landed(e2.at[1, b, :, w], pairsem(s_c2, 1, b))
 
         def total(i, _):
             r = rows(r_own + i * 48, 48)
             q = rows(i * 48, 48)
-            value = half[b, r, :] + (e2[0, b, q, :].astype(F32) + e2[1, b, q, :].astype(F32))
-            half[b, r, :] = value
-            f1[b, q, :] = value.astype(BF16)
+            value = half[b, r, w] + (e2[0, b, q, w].astype(F32) + e2[1, b, q, w].astype(F32))
+            half[b, r, w] = value
+            f1[b, q, w] = value.astype(BF16)
             return 0
 
         lax.fori_loop(0, 2, total, 0)
-        send(f1.at[b], f2.at[b], pairsem(s_f, b), xpart)
+        send(f1.at[b, :, w], f2.at[b, :, w], pairsem(s_f, b), xpart)
 
     def block(index):
         return (chip * 2 + SLAB_SHIFT[index] + 16) % 16
@@ -214,21 +233,29 @@
         return rows(base + ((yy + 4) % 4) * 96 + i * 48, 48)
 
     def send_spot(b, where, sem, device):
-        send(amp.at[b, where], amp.at[b, where], sem, device)
+        send(amp.at[b, where, wide(b)], amp.at[b, where, wide(b)], sem, device)
 
     def stage_u(b):
         here = spot(y)
         if b < N_PAIR:
-            landed(f2.at[b], pairsem(s_f, b))
+            landed(f2.at[b, :, wide(b)], pairsem(s_f, b))
             first = base + r_own
             within = first % 256
-            step = lax.broadcasted_iota(jnp.int32, (96, 128), 0) + within
+            group = first // 256
+            after = jnp.minimum(group + 1, 2)
+            step = lax.broadcasted_iota(jnp.int32, (96, 256), 0) + within
+            down = vcol[rows(within, 96), :]
+            down = jnp.concatenate([down, down], axis=1)
             for j, (left, right, k) in enumerate(BATCHES[b]):
-                e_row = block(left) * 3 + first // 256
-                e_next = block(left) * 3 + jnp.minimum(first // 256 + 1, 2)
-                row_e = vcol[rows(within, 96), :] - jnp.where(step < 256, occ_e[e_row], occ_e[e_next])
-                row_e = jnp.concatenate([row_e, row_e], axis=1)
-                col_e = virt[...] - occ_e[block(right) * 3 + k]
+                def energy(which, slots):
+                    first_e = occ_e[block(which) * 3 + slots[0]]
+                    return jnp.where(step < 256, first_e, occ_e[block(which) * 3 + slots[1]])
+                if k == PACKED:
+                    row_e = down - energy(left, (jnp.minimum(group + 1, 2), jnp.minimum(after + 1, 2)))
+                    col_e = virt[...] - energy(right, (1 + group // 2, 1 + after // 2))
+                else:
+                    row_e = down - energy(left, (group, after))
+                    col_e = virt[...] - occ_e[block(right) * 3 + k]
                 lanes = slice(j * 256, j * 256 + 256)
                 value = half[b, rows(r_own, 96), lanes] + f2[b, :, lanes].astype(F32)
                 amp[b, here, lanes] = (value / (row_e + col_e)).astype(BF16)
@@ -240,16 +267,18 @@
         send_spot(b, here, pairsem(s_ay, 1, b), ydn)
 
     def stage_w(b):
-        landed(amp.at[b, spot(y - 1)], pairsem(s_ay, 0, b))
+        w = wide(b)
+        landed(amp.at[b, spot(y - 1), w], pairsem(s_ay, 0, b))
         send_spot(b, halfspot(y - 1, 0), pairsem(s_fw, 0, b), yup)
-        landed(amp.at[b, spot(y + 1)], pairsem(s_ay, 1, b))
+        landed(amp.at[b, spot(y + 1), w], pairsem(s_ay, 1, b))
         send_spot(b, halfspot(y + 1, 1), pairsem(s_fw, 1, b), ydn)
 
     def stage_y(b):
-        landed(amp.at[b, halfspot(y + 2, 0)], pairsem(s_fw, 0, b))
-        landed(amp.at[b, halfspot(y + 2, 1)], pairsem(s_fw, 1, b))
+        w = wide(b)
+        landed(amp.at[b, halfspot(y + 2, 0), w], pairsem(s_fw, 0, b))
+        landed(amp.at[b, halfspot(y + 2, 1), w], pairsem(s_fw, 1, b))
         part = rows(base, 384)
-        send(amp.at[b, part], amp.at[b, part], pairsem(s_sib, b), sibling)
+        send(amp.at[b, part, w], amp.at[b, part, w], pairsem(s_sib, b), sibling)
 
     def cols(k):
         return slice(k * 256, k * 256 + 256)
@@ -260,6 +289,22 @@
     def turned(b, s):
         return lambda k: lax.dot_general(
             amp[b, :, cols(k)], slab[s], (((0,), (0,)), ((), ())), preferred_element_type=F32)
+
+    def diagonal(b):
+        def term(k):
+            if k == 0:
+                return lax.dot_general(
+                    amp[b, :, 0:256], slab[b], (((0,), (0,)), ((), ())), preferred_element_type=F32)
+            low = jnp.dot(amp[b, cols(k), 0:256], slab[b, 0:256, :], preferred_element_type=F32)
+            mid = jnp.dot(amp[b, cols(k - 1), 256:512], slab[b, 256:512, :], preferred_element_type=F32)
+            if k == 1:
+                high = lax.dot_general(
+                    amp[b, 256:512, 256:512], slab[b, 512:768, :], (((0,), (0,)), ((), ())),
+                    preferred_element_type=F32)
+            else:
+                high = jnp.dot(amp[b, 512:768, 256:512], slab[b, 512:768, :], preferred_element_type=F32)
+            return low + mid + high
+        return term
 
     def turned_unit(j, s):
         return lambda k: lax.dot_general(
@@ -280,10 +325,13 @@
             value = value + term(k)
         return value
 
+    def accumulate_one(which, terms, first, k):
+        value = total_of(terms, k)
+        gam[which, cols(k), :] = value if first else gam[which, cols(k), :] + value
+
     def accumulate(which, terms, first):
         for k in range(3):
-            value = total_of(terms, k)
-            gam[which, cols(k), :] = value if first else gam[which, cols(k), :] + value
+            accumulate_one(which, terms, first, k)
 
     def hand_back(k):
         bsend[0, cols(k), :] = total_of(
@@ -295,36 +343,51 @@
              (s_back.at[0, 1, k], s_back.at[1, core, k]), (up2, a))
 
     def stage_z(b):
-        landed(amp.at[b, rows(384 - base, 384)], pairsem(s_sib, b))
-
-    def stage_a(_):
-        accumulate(0, [plain(0, 0), turned(2, 1)], True)
-        accumulate(1, [plain(2, 0), plain(1, 1)], True)
-
-    def stage_c(_):
-        accumulate(0, [units(0, 2), units(2, 4)], False)
-        accumulate(1, [units(1, 2)], False)
+        landed(amp.at[b, rows(384 - base, 384), wide(b)], pairsem(s_sib, b))
+
+    def stage_a(which):
+        accumulate(which, [plain(2, 0), diagonal(1)] if which else [diagonal(0), turned(2, 1)], True)
+
+    def stage_c(which):
+        accumulate(which, [units(1, 2)] if which else [units(0, 2), units(2, 4)], False)
+
+    def keep(which, k):
+        return pltpu.make_async_copy(gam.at[which, cols(k)], out.at[cols(k), mine], s_out.at[2, k])
+
+    def hand_over(which, k):
+        return remote(gam.at[which, cols(k)], out.at[cols(k), mine], pairsem(s_out, k), sibling)
+
+    def stage_d(b):
+        which = 1 if b == 7 else 0
+        for k in range(3):
+            need(5 if b == 8 else 3, k)
+        for k in range(3):
+            accumulate_one(which, [plain(7, 3) if b == 7 else turned(8, 5)], False, k)
+
+            @pl.when(core == which)
+            def _():
+                keep(which, k).start()
+
+            @pl.when(core != which)
+            def _():
+                hand_over(which, k).start()
 
     stages = dict(P=stage_p, Q=stage_q, R=stage_r, T=stage_t, U=stage_u, W=stage_w, Y=stage_y, Z=stage_z,
-                  N=stage_n, B=hand_back, A=stage_a, C=stage_c)
+                  N=stage_n, B=hand_back, A=stage_a, C=stage_c, D=stage_d)
     for stage, b in ORDER:
         stages[stage](b)
-    for k in range(3):
-        need(5, k)
-    locals_ = []
-    for k in range(3):
-        for which, terms in ((0, [turned(8, 5)]), (1, [plain(7, 3)])):
-            gam[which, cols(k), :] = gam[which, cols(k), :] + total_of(terms, k)
-        send(gam.at[1 - core, cols(k)], out.at[cols(k), mine], pairsem(s_out, k), sibling)
-        copy = pltpu.make_async_copy(gam.at[core, cols(k)], out.at[cols(k), mine], s_out.at[2, k])
-        copy.start()
-        locals_.append(copy)
     for k in range(3):
         landed(out.at[cols(k), other], pairsem(s_out, k))
         for j in range(2):
             landed(back.at[cols(k), j * 768:j * 768 + 768], (s_back.at[0, 0, k], s_back.at[1, j, k]))
-    for copy in locals_:
-        copy.wait()
+        for which in range(2):
+            @pl.when(core == which)
+            def _():
+                keep(which, k).wait()
+
+            @pl.when(core != which)
+            def _():
+                hand_over(which, k).wait_send()
     for i in range(12 - AHEAD, 12):
         for d in range(2):
             chunks[d, i].wait_send()
@@ -340,13 +403,14 @@
         kernel,
         out_shape=(jax.ShapeDtypeStruct((768, 1536), F32), jax.ShapeDtypeStruct((768, 1536), BF16)),
         in_specs=[
-            pl.BlockSpec(memory_space=pltpu.VMEM),
+            pl.BlockSpec(memory_space=pl.ANY),
             pl.BlockSpec(memory_space=pltpu.SMEM),
             pl.BlockSpec(memory_space=pltpu.SMEM),
             pl.BlockSpec(memory_space=pltpu.VMEM),
         ],
         out_specs=(pl.BlockSpec(memory_space=pl.ANY), pl.BlockSpec(memory_space=pl.ANY)),
         scratch_shapes=[
+            vmem((768, 1536), BF16),
             vmem((768, 768), BF16),
             vmem((6, 768, 768), BF16),
             vmem((3, 384, 768), F32),
@@ -374,6 +438,7 @@
             dma((2,)),
             dma((2, 2, 3)),
             dma((3, 3)),
+            dma,
         ],
         compiler_params=pltpu.CompilerParams(
             collective_id=0, has_side_effects=True, vmem_limit_bytes=62 * 2**20),

time: 135 us -> 130 us (0.963)
  Pallas kernels: 129 us -> 124 us
    pallas_call x1, Pallas kernels: 129 us -> 124 us  [per_device(): pl.pallas_call(kernel, out_shape=(jax.ShapeDtypeStruct((768, 1536), F32),...]
where the time goes in v3:
time: 130 us
  Pallas kernels  124 us (95%)
  other arithmetic  5.99 us (5%)
    pallas_call x1, Pallas kernels, per_device(): pl.pallas_call(kernel, out_shape=(jax.ShapeDtypeStruct((768, 1536), F32),...  124 us
    add x1, other arithmetic, per_device(): return (partial + shares.astype(F32)).reshape(3, 256, 1536)  5.99 us

profile of v3, /device:TPU:1, one launch (start us, length us, event | category | flops | bytes accessed | tf_op | source)
XLA Modules:
  0.0 129.6 jit_solution(1501744501904495679)
XLA Ops:
  0.0 123.6 %window_gamma.1 = (f32[768,1536]{1,0:T(8,128)}, bf16[768,1536]{1,0:T(8,128)(2,1)}) custom-call(bf16[768,1536]{1,0:T(8,128)(2,1)} %bitcast.3, s32[16]{0:T(128)} %sizes.1, f32[48]{0:T(128)} %occ_e.1, f32[1,256]{1,0:T(1,128)} %bitcast.4), custom_call_target="tpu_custom_call" | custom-call | tf_op jit(solution)/shard_map/window_gamma/pallas_call | solution.py:402
  123.7 6.0 %convert_add_fusion = f32[768,1536]{1,0:T(8,128)} fusion(f32[768,1536]{1,0:T(8,128)} %get-tuple-element.7, bf16[768,1536]{1,0:T(8,128)(2,1)} %get-tuple-element.8), kind=kLoop, calls=%fused_computation | loop fusion | flops 2359296 | bytes 11796480 | tf_op jit(solution)/shard_map/add | solution.py:447

commit v4 on v3

--- a/solution.py
+++ b/solution.py
@@ -97,24 +97,31 @@
         return 0
 
     load.wait()
-    lax.fori_loop(0, 12, mask_other, 0)
     lax.fori_loop(0, 12, mask_mine, 0)
     pl.semaphore_wait(barrier, len(partners))
 
-    def send_chunk(i):
+    def chunk_copy(d, i):
         part = slice(i % 6 * 128, i % 6 * 128 + 128)
-        for d, (which, index, chip2) in enumerate((
-                (1 - i // 6, 2 + i // 6, up2), (i // 6, 4 + i // 6, dn2))):
-            chunk = remote(slab.at[which, part], slab.at[index, part], pairsem(s_slab, d, i), (chip2 + core, a))
-            chunk.start()
-            chunks[d, i] = chunk
+        which, index, chip2 = (1 - i // 6, 2 + i // 6, up2) if d == 0 else (i // 6, 4 + i // 6, dn2)
+        return remote(slab.at[which, part], slab.at[index, part], pairsem(s_slab, d, i), (chip2 + core, a))
+
+    def first_chunk(which, i):
+        part = slice(i * 128, i * 128 + 128)
+        chip2 = up2 * which + dn2 * (1 - which)
+        remote(slab.at[which, part], slab.at[4 - 2 * which, part], pairsem(s_slab, 1 - which, i),
+               (chip2 + core, a)).start()
 
     chunks = {}
+    for i in range(AHEAD):
+        first_chunk(core, i)
+    lax.fori_loop(0, 12, mask_other, 0)
     send(swap.at[0:256], slab.at[core, 0:256], pairsem(s_swap, 0), sibling)
     send(swap.at[256:768], slab.at[core, 256:768], pairsem(s_swap, 1), sibling)
     landed(slab.at[1 - core, 0:256], pairsem(s_swap, 0))
     for i in range(AHEAD):
-        send_chunk(i)
+        first_chunk(1 - core, i)
+        for d in range(2):
+            chunks[d, i] = chunk_copy(d, i)
 
     column = jnp.broadcast_to(virt[...], (128, 256)).T
     vcol[0:256, :] = column
@@ -134,7 +141,8 @@
     def stage_n(i):
         for d in range(2):
             chunks[d, i].wait_send()
-        send_chunk(i + AHEAD)
+            chunks[d, i + AHEAD] = chunk_copy(d, i + AHEAD)
+            chunks[d, i + AHEAD].start()
 
     base = core * 384
     r_own = y * 96
@@ -393,6 +401,10 @@
             chunks[d, i].wait_send()
     for copy in pending + list(gives.values()):
         copy.wait_send()
+
+
+def add_shares(partial, shares, out):
+    out[...] = partial[...] + shares[...].astype(F32)
 
 
 def per_device(orbital_b, block_size, occ_energy, virt_energy):
@@ -444,7 +456,17 @@
             collective_id=0, has_side_effects=True, vmem_limit_bytes=62 * 2**20),
         name="window_gamma",
     )(block, block_size, occ_energy, virt_energy.reshape(1, 256))
-    return (partial + shares.astype(F32)).reshape(3, 256, 1536)
+    step = pl.BlockSpec((96, 1536), lambda i: (i, 0))
+    total = pl.pallas_call(
+        add_shares,
+        out_shape=jax.ShapeDtypeStruct((768, 1536), F32),
+        grid=(8,),
+        in_specs=[step, step],
+        out_specs=step,
+        compiler_params=pltpu.CompilerParams(vmem_limit_bytes=62 * 2**20),
+        name="add_shares",
+    )(partial, shares)
+    return total.reshape(3, 256, 1536)
 
 
 def solution(mesh):

time: 130 us -> 130 us (level)
  other arithmetic: 5.99 us -> 0 us
  Pallas kernels: 124 us -> 129 us
    pallas_call x0 -> x1, Pallas kernels: none -> 7.45 us  [per_device(): pl.pallas_call(add_shares, out_shape=jax.ShapeDtypeStruct((768, 1536), F3...]
    add x1 -> x0, other arithmetic: 5.99 us -> none  [per_device(): return (partial + shares.astype(F32)).reshape(3, 256, 1536)]
    pallas_call x1, Pallas kernels: 124 us -> 122 us  [per_device(): pl.pallas_call(kernel, out_shape=(jax.ShapeDtypeStruct((768, 1536), F32),...]
where the time goes in v4:
time: 130 us; the launch traced here: 129 us
  Pallas kernels  129 us (99%)
    pallas_call x1, Pallas kernels, per_device(): pl.pallas_call(kernel, out_shape=(jax.ShapeDtypeStruct((768, 1536), F32),...  122 us
    pallas_call x1, Pallas kernels, per_device(): pl.pallas_call(add_shares, out_shape=jax.ShapeDtypeStruct((768, 1536), F3...  7.45 us

profile of v4, /device:TPU:1, one launch (start us, length us, event | category | flops | bytes accessed | tf_op | source)
XLA Modules:
  0.0 129.3 jit_solution(5245219431287242938)
XLA Ops:
  0.0 121.9 %window_gamma.1 = (f32[768,1536]{1,0:T(8,128)}, bf16[768,1536]{1,0:T(8,128)(2,1)}) custom-call(bf16[768,1536]{1,0:T(8,128)(2,1)} %bitcast.3, s32[16]{0:T(128)} %sizes.1, f32[48]{0:T(128)} %occ_e.1, f32[1,256]{1,0:T(1,128)} %bitcast.4), custom_call_target="tpu_custom_call" | custom-call | tf_op jit(solution)/shard_map/window_gamma/pallas_call | solution.py:414
  121.9 7.4 %add_shares.1 = f32[768,1536]{1,0:T(8,128)} custom-call(f32[768,1536]{1,0:T(8,128)} %get-tuple-element.7.partial, bf16[768,1536]{1,0:T(8,128)(2,1)} %get-tuple-element.8.shares), custom_call_target="tpu_custom_call" | custom-call | tf_op jit(solution)/shard_map/add_shares/pallas_call | solution.py:460

commit v5 on v4

--- a/solution.py
+++ b/solution.py
@@ -401,10 +401,6 @@
             chunks[d, i].wait_send()
     for copy in pending + list(gives.values()):
         copy.wait_send()
-
-
-def add_shares(partial, shares, out):
-    out[...] = partial[...] + shares[...].astype(F32)
 
 
 def per_device(orbital_b, block_size, occ_energy, virt_energy):
@@ -456,17 +452,7 @@
             collective_id=0, has_side_effects=True, vmem_limit_bytes=62 * 2**20),
         name="window_gamma",
     )(block, block_size, occ_energy, virt_energy.reshape(1, 256))
-    step = pl.BlockSpec((96, 1536), lambda i: (i, 0))
-    total = pl.pallas_call(
-        add_shares,
-        out_shape=jax.ShapeDtypeStruct((768, 1536), F32),
-        grid=(8,),
-        in_specs=[step, step],
-        out_specs=step,
-        compiler_params=pltpu.CompilerParams(vmem_limit_bytes=62 * 2**20),
-        name="add_shares",
-    )(partial, shares)
-    return total.reshape(3, 256, 1536)
+    return (partial + shares.astype(F32)).reshape(3, 256, 1536)
 
 
 def solution(mesh):

time: 130 us -> 128 us (0.985)
  Pallas kernels: 129 us -> 122 us
  other arithmetic: 0 us -> 5.99 us
    pallas_call x1 -> x0, Pallas kernels: 7.45 us -> none  [per_device(): pl.pallas_call(add_shares, out_shape=jax.ShapeDtypeStruct((768, 1536), F3...]
    add x0 -> x1, other arithmetic: none -> 5.99 us  [per_device(): return (partial + shares.astype(F32)).reshape(3, 256, 1536)]
where the time goes in v5:
time: 128 us
  Pallas kernels  122 us (95%)
  other arithmetic  5.99 us (5%)
    pallas_call x1, Pallas kernels, per_device(): pl.pallas_call(kernel, out_shape=(jax.ShapeDtypeStruct((768, 1536), F32),...  122 us
    add x1, other arithmetic, per_device(): return (partial + shares.astype(F32)).reshape(3, 256, 1536)  5.99 us

profile of v5, /device:TPU:1, one launch (start us, length us, event | category | flops | bytes accessed | tf_op | source)
XLA Modules:
  0.0 127.9 jit_solution(6760647570831892461)
XLA Ops:
  0.0 121.9 %window_gamma.1 = (f32[768,1536]{1,0:T(8,128)}, bf16[768,1536]{1,0:T(8,128)(2,1)}) custom-call(bf16[768,1536]{1,0:T(8,128)(2,1)} %bitcast.3, s32[16]{0:T(128)} %sizes.1, f32[48]{0:T(128)} %occ_e.1, f32[1,256]{1,0:T(1,128)} %bitcast.4), custom_call_target="tpu_custom_call" | custom-call | tf_op jit(solution)/shard_map/window_gamma/pallas_call | solution.py:410
  121.9 6.0 %convert_add_fusion = f32[768,1536]{1,0:T(8,128)} fusion(f32[768,1536]{1,0:T(8,128)} %get-tuple-element.7, bf16[768,1536]{1,0:T(8,128)(2,1)} %get-tuple-element.8), kind=kLoop, calls=%fused_computation | loop fusion | flops 2359296 | bytes 11796480 | tf_op jit(solution)/shard_map/add | solution.py:455
